TPU v7x, 32 devices: a whole 2x2x4 slice. The times are simulated.
32 devices in a mesh: grp: 2 (over x), ex: 16 (over z, y, core).
Axes of the slice: x: 2, y: 2, z: 4, core: 2. Of those that a mesh axis runs over, the one named last changes fastest.
Arguments:
- train_features: bfloat16 [2, 20480, 4096], P(None, ('grp', 'ex')), parts along dimension 1, may hold values from -400 to 400
- test_features: bfloat16 [2, 256, 4096], P(None, ('grp', 'ex')), parts along dimension 1, may hold values from -64 to 64
Outputs:
- influence: bfloat16 [20480, 128], P(('grp', 'ex')), parts along dimension 0
There are 2 independent parts, one for each index of `grp`. A program takes and returns all parts, laid end to end along the dimension named above; each array names one. Nothing has to cross between parts.
All inputs are finite; a program needn't handle non-finite values.
Results may differ from a plain program's by a relative error of at most 0.0068.
Values may be sent and summed in bfloat16 or wider, within the bound.
A program may use at most 128 MiB of HBM per device.

v0:
```python
import functools

import jax
import jax.numpy as jnp
from jax import lax
from jax.experimental import pallas as pl
from jax.experimental.pallas import tpu as pltpu
from jax.sharding import PartitionSpec as P

K = 64
FEATURES = K * K
LANES = 128
TILES = 16
PARTS = 4
WIDE = 256


def dot(a, b, dims=((1,), (0,))):
    return lax.dot_general(a, b, (dims, ((), ())), preferred_element_type=jnp.float32)


def loop(count, step):
    def run(index, carry):
        step(index)
        return carry

    lax.fori_loop(0, count, run, 0)


def fold(acc):
    half = acc[:LANES, :LANES] + acc[LANES:, LANES:]
    top, low = half[:K], half[K:]
    return top + pltpu.roll(low, K, 1), pltpu.roll(top, K, 1) + low


def kernel(
    n, total_rows, train_hbm, test_ref, out_ref,
    x, xt, acc_in, acc_out, gathered, queries, right, both, scores,
    stats, reduce_buf, reduced, state, power_buf,
    load_sem, gsend, grecv, rsend, rrecv, asend, arecv, psend, precv,
):
    layers, rows, _ = x.shape
    me = lax.axis_index("ex")
    row_blocks = rows // LANES
    query_blocks = queries.shape[1]
    owners = min(n, TILES)
    tile = 2 * K // owners
    part = FEATURES // PARTS

    def load(layer, piece):
        columns = pl.ds(piece * part, part)
        return pltpu.make_async_copy(
            train_hbm.at[layer, :, columns], x.at[layer, :, columns], load_sem.at[layer, piece]
        )

    def remote(src, dst, send, recv, target):
        return pltpu.make_async_remote_copy(
            src_ref=src, dst_ref=dst, send_sem=send, recv_sem=recv,
            device_id={"ex": target}, device_id_type=pl.DeviceIdType.MESH,
        )

    for layer in range(layers):
        for piece in range(PARTS):
            load(layer, piece).start()

    barrier = pltpu.get_barrier_semaphore()

    def greet(offset):
        pl.semaphore_signal(
            barrier, inc=1, device_id={"ex": lax.rem(me + offset + 1, n)},
            device_id_type=pl.DeviceIdType.MESH,
        )

    loop(n - 1, greet)
    gathered[me] = jnp.concatenate(
        [test_ref[layer].astype(jnp.float32) for layer in range(layers)], axis=0
    ).astype(jnp.bfloat16)
    pl.semaphore_wait(barrier, n - 1)

    groups = n // 4
    mine_a, mine_r = me // 4, me % 4
    mine_b, mine_c = mine_r // 2, mine_r % 2
    across = mine_a * 4 + (1 - mine_b) * 2 + mine_c
    beside = mine_a * 4 + mine_b * 2 + (1 - mine_c)

    def pass_on(slot, target, index):
        return remote(gathered.at[slot], gathered.at[slot], gsend.at[index], grecv.at[slot], target)

    def first(offset):
        pass_on(me, lax.rem(mine_a + offset + 1, groups) * 4 + mine_r, offset).start()

    loop(groups - 1, first)

    def forward_across():
        pass_on(me, across, groups - 1).start()

        def step(offset):
            slot = lax.rem(mine_a + groups - offset - 1, groups) * 4 + mine_r
            pass_on(slot, across, groups + offset).wait_recv()
            pass_on(slot, across, groups + offset).start()

        loop(groups - 1, step)

    def forward_beside():
        def own(offset):
            slot = lax.rem(mine_a + groups - offset, groups) * 4 + mine_r
            pass_on(slot, beside, 2 * groups - 1 + offset).start()

        loop(groups, own)

        def other(offset):
            slot = lax.rem(mine_a + groups - offset, groups) * 4 + (1 - mine_b) * 2 + mine_c
            pass_on(slot, beside, 3 * groups - 1 + offset).wait_recv()
            pass_on(slot, beside, 3 * groups - 1 + offset).start()

        loop(groups, other)

    def outer_stats(layer):
        acc_out[...] = jnp.zeros_like(acc_out)
        for piece in range(PARTS):
            load(layer, piece).wait()

            def step(index, piece=piece):
                start = pl.multiple_of(piece * part + index * WIDE, WIDE)
                block = x[layer, :, pl.ds(start, WIDE)]
                turned = block.T
                acc_out[...] += dot(turned, block)
                for r in range(row_blocks):
                    xt[pl.ds(pl.multiple_of(r * FEATURES + start, WIDE), WIDE), :] = turned[
                        :, r * LANES : (r + 1) * LANES
                    ].astype(jnp.float32)

            loop(part // WIDE, step)

    def inner_stats(layer):
        acc_in[...] = jnp.zeros_like(acc_in)

        def step(index):
            block = jnp.concatenate(
                [
                    jnp.concatenate(
                        [
                            xt[pl.ds(r * FEATURES + index * 4 + u, K, stride=K), :].astype(jnp.bfloat16)
                            for r in range(row_blocks)
                        ],
                        axis=1,
                    )
                    for u in range(4)
                ],
                axis=0,
            )
            acc_in[...] += dot(block, block, ((1,), (1,)))

        loop(K // 4, step)

    lane = lax.broadcasted_iota(jnp.int32, (K, LANES), 1)
    sub = lax.broadcasted_iota(jnp.int32, (K, LANES), 0)
    low_half = lane < K

    for layer in range(layers):
        outer_stats(layer)
        if layer == 0:
            forward_across()
        else:
            forward_beside()
        inner_stats(layer)
        stats[layer * K : (layer + 1) * K, :] = jnp.where(
            low_half, fold(acc_in[...])[0], fold(acc_out[...])[1]
        )

    def tile_rows(owner):
        return pl.ds(pl.multiple_of(owner * tile, tile), tile)

    def to_owner(owner):
        return remote(stats.at[tile_rows(owner)], reduce_buf.at[me], rsend.at[owner], rrecv.at[me], owner)

    def only(condition, action):
        if owners == n:
            action()
        else:
            pl.when(condition)(action)

    def send_tile(offset):
        owner = lax.rem(me + offset + 1, n)
        only(owner < owners, lambda: to_owner(owner).start())

    loop(n - 1, send_tile)

    def from_owner(owner, target, index):
        return remote(reduced.at[tile_rows(owner)], reduced.at[tile_rows(owner)], asend.at[index], arecv.at[owner], target)

    def reduce_own():
        reduce_buf[me] = stats[tile_rows(me), :]

        def arrive(offset):
            source = lax.rem(me + n - offset - 1, n)
            remote(reduce_buf.at[source], reduce_buf.at[source], rsend.at[0], rrecv.at[source], source).wait_recv()

        loop(n - 1, arrive)
        total = reduce_buf[0]
        for source in range(1, n):
            total = total + reduce_buf[source]
        reduced[tile_rows(me), :] = total / total_rows

        def spread(offset):
            from_owner(me, lax.rem(me + offset + 1, n), offset).start()

        loop(n - 1, spread)

    only(me < owners, reduce_own)

    def arrive_beside(offset):
        slot = offset * 2 + (1 - mine_c)
        pass_on(slot, beside, 0).wait_recv()

    loop(n // 2, arrive_beside)

    per_block = LANES // 8

    def turn_queries(index):
        start = pl.multiple_of(index * LANES, LANES)
        for block in range(query_blocks):
            values = gathered[block * per_block : (block + 1) * per_block, :, pl.ds(start, LANES)].astype(jnp.float32)
            for layer in range(layers):
                turned = values[:, layer * 8 : (layer + 1) * 8, :].reshape(LANES, LANES).T
                queries[layer, block, pl.ds(start, LANES), :] = turned.astype(jnp.bfloat16)

    loop(FEATURES // LANES, turn_queries)

    def arrive_total(offset):
        owner = lax.rem(me + n - offset - 1, n)
        only(owner < owners, lambda: from_owner(owner, owner, 0).wait_recv())

    loop(n - 1, arrive_total)

    for layer in range(layers):
        value = reduced[layer * K : (layer + 1) * K, :]
        diagonal = (lane == sub) | (lane == sub + K)
        on = jnp.where(diagonal, value, 0.0)
        trace_in = jnp.sum(jnp.where(low_half, on, 0.0))
        trace_out = jnp.sum(jnp.where(low_half, 0.0, on))
        damping = 0.1 * jnp.where(low_half, trace_in, trace_out) / K
        state[layer] = jnp.where(diagonal, value + damping, value)

    def sweep(k):
        at_low, at_high, at_row = lane == k, lane == k + K, sub == k
        at_column = at_low | at_high
        for layer in range(layers):
            value = state[layer]
            row = state[layer, pl.ds(k, 1), :]
            column = jnp.where(
                low_half,
                jnp.sum(jnp.where(at_low, value, 0.0), axis=1, keepdims=True),
                jnp.sum(jnp.where(at_high, value, 0.0), axis=1, keepdims=True),
            )
            pivot = jnp.where(
                low_half[:1],
                jnp.sum(jnp.where(at_low[:1], row, 0.0), axis=1, keepdims=True),
                jnp.sum(jnp.where(at_high[:1], row, 0.0), axis=1, keepdims=True),
            )
            inverse = 1.0 / pivot
            scaled = row * inverse
            new = jnp.where(at_column, column * inverse, value - column * scaled)
            state[layer] = jnp.where(at_row, jnp.where(at_column, -inverse, scaled), new)

    loop(K, sweep)

    scores[...] = jnp.zeros_like(scores)
    for layer in range(layers):
        inverse = -state[layer]
        high = inverse.astype(jnp.bfloat16).astype(jnp.float32)
        rest = inverse - high
        right_pair = jnp.where(low_half, pltpu.roll(high, K, 1), rest).astype(jnp.bfloat16)
        left_pair = jnp.where(low_half, high, pltpu.roll(rest, K, 1)).astype(jnp.bfloat16)
        left_four = jnp.concatenate([left_pair, left_pair], axis=1)
        for block in range(query_blocks):

            def apply_right(index, layer=layer, block=block):
                start = pl.multiple_of(index * 4 * K, 4 * K)
                wide = [queries[layer, block, pl.ds(start + u * K, K), :] for u in range(4)]
                wide = jnp.concatenate(wide, axis=1)
                result = dot(right_pair, jnp.concatenate([wide, wide], axis=0))
                for u in range(4):
                    right[pl.ds(pl.multiple_of(start + u * K, K), K), :] = result[:, u * LANES : (u + 1) * LANES]

            loop(K // 4, apply_right)

            def apply_left(index):
                value = jnp.concatenate(
                    [right[pl.ds(index * 4 + u, K, stride=K), :] for u in range(4)], axis=1
                )
                upper = value.astype(jnp.bfloat16)
                lower = (value - upper.astype(jnp.float32)).astype(jnp.bfloat16)
                result = dot(left_four, jnp.concatenate([upper, upper, lower, lower], axis=0))
                for u in range(4):
                    both[pl.ds(index * 4 + u, K, stride=K), :] = result[:, u * LANES : (u + 1) * LANES]

            loop(K // 4, apply_left)

            def score(index, layer=layer, block=block):
                start = pl.multiple_of(index * 512, 512)
                scores[block] += dot(
                    x[layer, :, pl.ds(start, 512)], both[pl.ds(start, 512), :].astype(jnp.bfloat16)
                )

            loop(FEATURES // 512, score)

    for block in range(query_blocks):
        value = scores[block]
        power_buf[me, :, block * LANES : (block + 1) * LANES] = jnp.broadcast_to(
            jnp.sum(value * value, axis=0, keepdims=True), (8, LANES)
        )

    def send_power(offset):
        target = lax.rem(me + offset + 1, n)
        remote(power_buf.at[me], power_buf.at[me], psend.at[offset], precv.at[me], target).start()

    loop(n - 1, send_power)

    def arrive_power(offset):
        source = lax.rem(me + n - offset - 1, n)
        remote(power_buf.at[source], power_buf.at[source], psend.at[0], precv.at[source], source).wait_recv()

    loop(n - 1, arrive_power)
    power = power_buf[0]
    for source in range(1, n):
        power = power + power_buf[source]
    scale = lax.rsqrt(power / total_rows + 1e-06)
    for block in range(query_blocks):
        columns = slice(block * LANES, (block + 1) * LANES)
        out_ref[:, columns] = (scores[block] * scale[:1, columns]).astype(out_ref.dtype)

    def sent_queries(index):
        pass_on(me, beside, index).wait_send()

    loop(n - 1, sent_queries)

    def sent_tile(offset):
        owner = lax.rem(me + offset + 1, n)
        only(owner < owners, lambda: to_owner(owner).wait_send())

    loop(n - 1, sent_tile)

    def sent_total():
        loop(n - 1, lambda offset: from_owner(me, beside, offset).wait_send())

    only(me < owners, sent_total)

    def sent_power(offset):
        remote(power_buf.at[me], power_buf.at[me], psend.at[offset], precv.at[me], beside).wait_send()

    loop(n - 1, sent_power)


def body(train_features, test_features):
    layers, rows, features = train_features.shape
    count = test_features.shape[1]
    n = lax.axis_size("ex")
    query_count = count * n
    query_blocks = query_count // LANES
    owners = min(n, TILES)
    f32, bf16 = jnp.float32, jnp.bfloat16
    dma = pltpu.SemaphoreType.DMA
    return pl.pallas_call(
        functools.partial(kernel, n, rows * n),
        out_shape=jax.ShapeDtypeStruct((rows, query_count), bf16),
        in_specs=[pl.BlockSpec(memory_space=pl.ANY), pl.BlockSpec(memory_space=pltpu.VMEM)],
        out_specs=pl.BlockSpec(memory_space=pltpu.VMEM),
        scratch_shapes=[
            pltpu.VMEM((layers, rows, features), bf16),
            pltpu.VMEM((rows // LANES * features, LANES), f32),
            pltpu.VMEM((WIDE, WIDE), f32),
            pltpu.VMEM((WIDE, WIDE), f32),
            pltpu.VMEM((n, layers * count, features), bf16),
            pltpu.VMEM((layers, query_blocks, features, LANES), bf16),
            pltpu.VMEM((features, LANES), f32),
            pltpu.VMEM((features, LANES), f32),
            pltpu.VMEM((query_blocks, rows, LANES), f32),
            pltpu.VMEM((layers * K, LANES), f32),
            pltpu.VMEM((n, layers * K // owners, LANES), f32),
            pltpu.VMEM((layers * K, LANES), f32),
            pltpu.VMEM((layers, K, LANES), f32),
            pltpu.VMEM((n, 8, query_count), f32),
            dma((layers, PARTS)),
            dma((n,)), dma((n,)), dma((n,)), dma((n,)),
            dma((n,)), dma((n,)), dma((n,)), dma((n,)),
        ],
        compiler_params=pltpu.CompilerParams(
            collective_id=0, has_side_effects=True, vmem_limit_bytes=60 * 1024 * 1024
        ),
    )(train_features, test_features)


def solution(mesh):
    in_specs = (P(None, ("grp", "ex"), None), P(None, ("grp", "ex"), None))
    out_specs = P(("grp", "ex"), None)
    return jax.shard_map(body, mesh=mesh, in_specs=in_specs, out_specs=out_specs, check_vma=False)
```

profile of v0, /device:TPU:0, one launch (start us, length us, event | category | flops | bytes accessed | tf_op | source)
XLA Modules:
  0.0 100.0 jit_solution(471349641557146603)
XLA Ops:
  0.0 98.4 %shard_map.28 = bf16[640,128]{1,0:T(8,128)(2,1)} custom-call(bf16[2,640,4096]{2,1,0:T(8,128)(2,1)} %train_hbm.1, bf16[2,8,4096]{2,1,0:T(8,128)(2,1)} %test_ref.1), custom_call_target="tpu_custom_call" | custom-call | tf_op jit(solution)/shard_map/pallas_call | solution.py:364
  98.4 1.6 %copy.4 = bf16[640,128]{1,0:T(8,128)(2,1)} copy(bf16[640,128]{1,0:T(8,128)(2,1)} %shard_map.28) | data formatting | bytes 327680
where the time goes:
time: 100 us
  Pallas kernels  98.4 us (98%)
  local copies, waits for them, and re-layouts  1.59 us (2%)
    pallas_call x1, Pallas kernels, body(): pl.pallas_call(functools.partial(kernel, n, rows * n), out_shape=jax.Shap...  98.4 us

commit v1 on v0

--- a/solution.py
+++ b/solution.py
@@ -13,6 +13,7 @@
 TILES = 16
 PARTS = 4
 WIDE = 256
+PITCH = K + 1
 
 
 def dot(a, b, dims=((1,), (0,))):
@@ -90,10 +91,10 @@
         pass_on(me, lax.rem(mine_a + offset + 1, groups) * 4 + mine_r, offset).start()
 
     loop(groups - 1, first)
+    pass_on(me, across, groups - 1).start()
+    pass_on(me, beside, 2 * groups - 1).start()
 
     def forward_across():
-        pass_on(me, across, groups - 1).start()
-
         def step(offset):
             slot = lax.rem(mine_a + groups - offset - 1, groups) * 4 + mine_r
             pass_on(slot, across, groups + offset).wait_recv()
@@ -103,10 +104,10 @@
 
     def forward_beside():
         def own(offset):
-            slot = lax.rem(mine_a + groups - offset, groups) * 4 + mine_r
-            pass_on(slot, beside, 2 * groups - 1 + offset).start()
-
-        loop(groups, own)
+            slot = lax.rem(mine_a + groups - offset - 1, groups) * 4 + mine_r
+            pass_on(slot, beside, 2 * groups + offset).start()
+
+        loop(groups - 1, own)
 
         def other(offset):
             slot = lax.rem(mine_a + groups - offset, groups) * 4 + (1 - mine_b) * 2 + mine_c
@@ -125,10 +126,12 @@
                 block = x[layer, :, pl.ds(start, WIDE)]
                 turned = block.T
                 acc_out[...] += dot(turned, block)
+                first_block = piece * (part // K) + index * (WIDE // K)
                 for r in range(row_blocks):
-                    xt[pl.ds(pl.multiple_of(r * FEATURES + start, WIDE), WIDE), :] = turned[
-                        :, r * LANES : (r + 1) * LANES
-                    ].astype(jnp.float32)
+                    for u in range(WIDE // K):
+                        xt[pl.ds((r * K + first_block + u) * PITCH, K), :] = turned[
+                            u * K : (u + 1) * K, r * LANES : (r + 1) * LANES
+                        ].astype(jnp.float32)
 
             loop(part // WIDE, step)
 
@@ -140,7 +143,7 @@
                 [
                     jnp.concatenate(
                         [
-                            xt[pl.ds(r * FEATURES + index * 4 + u, K, stride=K), :].astype(jnp.bfloat16)
+                            xt[pl.ds(r * K * PITCH + index * 4 + u, K, stride=PITCH), :].astype(jnp.bfloat16)
                             for r in range(row_blocks)
                         ],
                         axis=1,
@@ -159,11 +162,9 @@
 
     for layer in range(layers):
         outer_stats(layer)
+        inner_stats(layer)
         if layer == 0:
             forward_across()
-        else:
-            forward_beside()
-        inner_stats(layer)
         stats[layer * K : (layer + 1) * K, :] = jnp.where(
             low_half, fold(acc_in[...])[0], fold(acc_out[...])[1]
         )
@@ -185,6 +186,7 @@
         only(owner < owners, lambda: to_owner(owner).start())
 
     loop(n - 1, send_tile)
+    forward_beside()
 
     def from_owner(owner, target, index):
         return remote(reduced.at[tile_rows(owner)], reduced.at[tile_rows(owner)], asend.at[index], arecv.at[owner], target)
@@ -243,22 +245,16 @@
         state[layer] = jnp.where(diagonal, value + damping, value)
 
     def sweep(k):
-        at_low, at_high, at_row = lane == k, lane == k + K, sub == k
-        at_column = at_low | at_high
+        place = jnp.where(low_half, k, k + K)
+        at_column, at_row = lane == place, sub == k
         for layer in range(layers):
             value = state[layer]
             row = state[layer, pl.ds(k, 1), :]
-            column = jnp.where(
-                low_half,
-                jnp.sum(jnp.where(at_low, value, 0.0), axis=1, keepdims=True),
-                jnp.sum(jnp.where(at_high, value, 0.0), axis=1, keepdims=True),
+            column = jnp.take_along_axis(value, place, axis=1, mode="promise_in_bounds")
+            pivot = jnp.take_along_axis(
+                jnp.broadcast_to(row, (8, LANES)), place[:8], axis=1, mode="promise_in_bounds"
             )
-            pivot = jnp.where(
-                low_half[:1],
-                jnp.sum(jnp.where(at_low[:1], row, 0.0), axis=1, keepdims=True),
-                jnp.sum(jnp.where(at_high[:1], row, 0.0), axis=1, keepdims=True),
-            )
-            inverse = 1.0 / pivot
+            inverse = 1.0 / pivot[:1]
             scaled = row * inverse
             new = jnp.where(at_column, column * inverse, value - column * scaled)
             state[layer] = jnp.where(at_row, jnp.where(at_column, -inverse, scaled), new)
@@ -281,27 +277,28 @@
                 wide = jnp.concatenate(wide, axis=1)
                 result = dot(right_pair, jnp.concatenate([wide, wide], axis=0))
                 for u in range(4):
-                    right[pl.ds(pl.multiple_of(start + u * K, K), K), :] = result[:, u * LANES : (u + 1) * LANES]
+                    right[pl.ds((index * 4 + u) * PITCH, K), :] = result[:, u * LANES : (u + 1) * LANES]
 
             loop(K // 4, apply_right)
 
             def apply_left(index):
                 value = jnp.concatenate(
-                    [right[pl.ds(index * 4 + u, K, stride=K), :] for u in range(4)], axis=1
+                    [right[pl.ds(index * 4 + u, K, stride=PITCH), :] for u in range(4)], axis=1
                 )
                 upper = value.astype(jnp.bfloat16)
                 lower = (value - upper.astype(jnp.float32)).astype(jnp.bfloat16)
                 result = dot(left_four, jnp.concatenate([upper, upper, lower, lower], axis=0))
                 for u in range(4):
-                    both[pl.ds(index * 4 + u, K, stride=K), :] = result[:, u * LANES : (u + 1) * LANES]
+                    both[pl.ds(index * 4 + u, K, stride=PITCH), :] = result[:, u * LANES : (u + 1) * LANES]
 
             loop(K // 4, apply_left)
 
             def score(index, layer=layer, block=block):
                 start = pl.multiple_of(index * 512, 512)
-                scores[block] += dot(
-                    x[layer, :, pl.ds(start, 512)], both[pl.ds(start, 512), :].astype(jnp.bfloat16)
-                )
+                weights = [
+                    both[pl.ds((index * 8 + u) * PITCH, K), :].astype(jnp.bfloat16) for u in range(8)
+                ]
+                scores[block] += dot(x[layer, :, pl.ds(start, 512)], jnp.concatenate(weights, axis=0))
 
             loop(FEATURES // 512, score)
 
@@ -368,13 +365,13 @@
         out_specs=pl.BlockSpec(memory_space=pltpu.VMEM),
         scratch_shapes=[
             pltpu.VMEM((layers, rows, features), bf16),
-            pltpu.VMEM((rows // LANES * features, LANES), f32),
+            pltpu.VMEM((rows // LANES * K * PITCH, LANES), f32),
             pltpu.VMEM((WIDE, WIDE), f32),
             pltpu.VMEM((WIDE, WIDE), f32),
             pltpu.VMEM((n, layers * count, features), bf16),
             pltpu.VMEM((layers, query_blocks, features, LANES), bf16),
-            pltpu.VMEM((features, LANES), f32),
-            pltpu.VMEM((features, LANES), f32),
+            pltpu.VMEM((K * PITCH, LANES), f32),
+            pltpu.VMEM((K * PITCH, LANES), f32),
             pltpu.VMEM((query_blocks, rows, LANES), f32),
             pltpu.VMEM((layers * K, LANES), f32),
             pltpu.VMEM((n, layers * K // owners, LANES), f32),

time: 100 us -> 74.2 us (0.74)
  Pallas kernels: 98.4 us -> 72.5 us
    pallas_call x1, Pallas kernels: 98.4 us -> 72.5 us  [body(): pl.pallas_call(functools.partial(kernel, n, rows * n), out_shape=jax.Shap...]
where the time goes in v1:
time: 74.2 us; the launch traced here: 74.1 us
  Pallas kernels  72.5 us (98%)
  local copies, waits for them, and re-layouts  1.59 us (2%)
    pallas_call x1, Pallas kernels, body(): pl.pallas_call(functools.partial(kernel, n, rows * n), out_shape=jax.Shap...  72.5 us
    unnamed x1, local copies, waits for them, and re-layouts  1.59 us

profile of v1, /device:TPU:0, one launch (start us, length us, event | category | flops | bytes accessed | tf_op | source)
XLA Modules:
  0.0 74.1 jit_solution(1979100537296551295)
XLA Ops:
  0.0 72.5 %shard_map.28 = bf16[640,128]{1,0:T(8,128)(2,1)} custom-call(bf16[2,640,4096]{2,1,0:T(8,128)(2,1)} %train_hbm.1, bf16[2,8,4096]{2,1,0:T(8,128)(2,1)} %test_ref.1), custom_call_target="tpu_custom_call" | custom-call | tf_op jit(solution)/shard_map/pallas_call | solution.py:361
  72.5 1.6 %copy.4 = bf16[640,128]{1,0:T(8,128)(2,1)} copy(bf16[640,128]{1,0:T(8,128)(2,1)} %shard_map.28) | data formatting | bytes 327680

commit v2 on v1

--- a/solution.py
+++ b/solution.py
@@ -20,12 +20,13 @@
     return lax.dot_general(a, b, (dims, ((), ())), preferred_element_type=jnp.float32)
 
 
-def loop(count, step):
+def loop(count, step, together=1):
     def run(index, carry):
-        step(index)
+        for u in range(together):
+            step(index * together + u)
         return carry
 
-    lax.fori_loop(0, count, run, 0)
+    lax.fori_loop(0, count // together, run, 0)
 
 
 def fold(acc):
@@ -37,7 +38,7 @@
 def kernel(
     n, total_rows, train_hbm, test_ref, out_ref,
     x, xt, acc_in, acc_out, gathered, queries, right, both, scores,
-    stats, reduce_buf, reduced, state, power_buf,
+    stats, reduce_buf, reduced, power_buf,
     load_sem, gsend, grecv, rsend, rrecv, asend, arecv, psend, precv,
 ):
     layers, rows, _ = x.shape
@@ -133,7 +134,7 @@
                             u * K : (u + 1) * K, r * LANES : (r + 1) * LANES
                         ].astype(jnp.float32)
 
-            loop(part // WIDE, step)
+            loop(part // WIDE, step, 2)
 
     def inner_stats(layer):
         acc_in[...] = jnp.zeros_like(acc_in)
@@ -154,7 +155,7 @@
             )
             acc_in[...] += dot(block, block, ((1,), (1,)))
 
-        loop(K // 4, step)
+        loop(K // 4, step, 2)
 
     lane = lax.broadcasted_iota(jnp.int32, (K, LANES), 1)
     sub = lax.broadcasted_iota(jnp.int32, (K, LANES), 0)
@@ -235,6 +236,7 @@
 
     loop(n - 1, arrive_total)
 
+    states = []
     for layer in range(layers):
         value = reduced[layer * K : (layer + 1) * K, :]
         diagonal = (lane == sub) | (lane == sub + K)
@@ -242,14 +244,14 @@
         trace_in = jnp.sum(jnp.where(low_half, on, 0.0))
         trace_out = jnp.sum(jnp.where(low_half, 0.0, on))
         damping = 0.1 * jnp.where(low_half, trace_in, trace_out) / K
-        state[layer] = jnp.where(diagonal, value + damping, value)
-
-    def sweep(k):
+        states.append(jnp.where(diagonal, value + damping, value))
+
+    for k in range(K):
         place = jnp.where(low_half, k, k + K)
         at_column, at_row = lane == place, sub == k
         for layer in range(layers):
-            value = state[layer]
-            row = state[layer, pl.ds(k, 1), :]
+            value = states[layer]
+            row = value[k : k + 1]
             column = jnp.take_along_axis(value, place, axis=1, mode="promise_in_bounds")
             pivot = jnp.take_along_axis(
                 jnp.broadcast_to(row, (8, LANES)), place[:8], axis=1, mode="promise_in_bounds"
@@ -257,13 +259,11 @@
             inverse = 1.0 / pivot[:1]
             scaled = row * inverse
             new = jnp.where(at_column, column * inverse, value - column * scaled)
-            state[layer] = jnp.where(at_row, jnp.where(at_column, -inverse, scaled), new)
-
-    loop(K, sweep)
+            states[layer] = jnp.where(at_row, jnp.where(at_column, -inverse, scaled), new)
 
     scores[...] = jnp.zeros_like(scores)
     for layer in range(layers):
-        inverse = -state[layer]
+        inverse = -states[layer]
         high = inverse.astype(jnp.bfloat16).astype(jnp.float32)
         rest = inverse - high
         right_pair = jnp.where(low_half, pltpu.roll(high, K, 1), rest).astype(jnp.bfloat16)
@@ -279,7 +279,7 @@
                 for u in range(4):
                     right[pl.ds((index * 4 + u) * PITCH, K), :] = result[:, u * LANES : (u + 1) * LANES]
 
-            loop(K // 4, apply_right)
+            loop(K // 4, apply_right, 4)
 
             def apply_left(index):
                 value = jnp.concatenate(
@@ -291,16 +291,16 @@
                 for u in range(4):
                     both[pl.ds(index * 4 + u, K, stride=PITCH), :] = result[:, u * LANES : (u + 1) * LANES]
 
-            loop(K // 4, apply_left)
+            loop(K // 4, apply_left, 4)
 
             def score(index, layer=layer, block=block):
-                start = pl.multiple_of(index * 512, 512)
+                start = pl.multiple_of(index * 1024, 1024)
                 weights = [
-                    both[pl.ds((index * 8 + u) * PITCH, K), :].astype(jnp.bfloat16) for u in range(8)
+                    both[pl.ds((index * 16 + u) * PITCH, K), :].astype(jnp.bfloat16) for u in range(16)
                 ]
-                scores[block] += dot(x[layer, :, pl.ds(start, 512)], jnp.concatenate(weights, axis=0))
-
-            loop(FEATURES // 512, score)
+                scores[block] += dot(x[layer, :, pl.ds(start, 1024)], jnp.concatenate(weights, axis=0))
+
+            loop(FEATURES // 1024, score)
 
     for block in range(query_blocks):
         value = scores[block]
@@ -376,7 +376,6 @@
             pltpu.VMEM((layers * K, LANES), f32),
             pltpu.VMEM((n, layers * K // owners, LANES), f32),
             pltpu.VMEM((layers * K, LANES), f32),
-            pltpu.VMEM((layers, K, LANES), f32),
             pltpu.VMEM((n, 8, query_count), f32),
             dma((layers, PARTS)),
             dma((n,)), dma((n,)), dma((n,)), dma((n,)),

time: 74.2 us -> 57.3 us (0.77)
  Pallas kernels: 72.5 us -> 55.6 us
    pallas_call x1, Pallas kernels: 72.5 us -> 55.6 us  [body(): pl.pallas_call(functools.partial(kernel, n, rows * n), out_shape=jax.Shap...]
where the time goes in v2:
time: 57.3 us; the launch traced here: 57.2 us
  Pallas kernels  55.6 us (97%)
  local copies, waits for them, and re-layouts  1.59 us (3%)
    pallas_call x1, Pallas kernels, body(): pl.pallas_call(functools.partial(kernel, n, rows * n), out_shape=jax.Shap...  55.6 us
    unnamed x1, local copies, waits for them, and re-layouts  1.59 us

profile of v2, /device:TPU:0, one launch (start us, length us, event | category | flops | bytes accessed | tf_op | source)
XLA Modules:
  0.0 57.2 jit_solution(4612660175721397665)
XLA Ops:
  0.0 55.6 %shard_map.28 = bf16[640,128]{1,0:T(8,128)(2,1)} custom-call(bf16[2,640,4096]{2,1,0:T(8,128)(2,1)} %train_hbm.1, bf16[2,8,4096]{2,1,0:T(8,128)(2,1)} %test_ref.1), custom_call_target="tpu_custom_call" | custom-call | tf_op jit(solution)/shard_map/pallas_call | solution.py:361
  55.6 1.6 %copy.4 = bf16[640,128]{1,0:T(8,128)(2,1)} copy(bf16[640,128]{1,0:T(8,128)(2,1)} %shard_map.28) | data formatting | bytes 327680

commit v3 on v2

--- a/solution.py
+++ b/solution.py
@@ -46,6 +46,7 @@
     row_blocks = rows // LANES
     query_blocks = queries.shape[1]
     owners = min(n, TILES)
+    spread_out = 3 if n % 3 == 1 else 1
     tile = 2 * K // owners
     part = FEATURES // PARTS
 
@@ -73,7 +74,7 @@
             device_id_type=pl.DeviceIdType.MESH,
         )
 
-    loop(n - 1, greet)
+    loop(n - 1, greet, spread_out)
     gathered[me] = jnp.concatenate(
         [test_ref[layer].astype(jnp.float32) for layer in range(layers)], axis=0
     ).astype(jnp.bfloat16)
@@ -134,7 +135,7 @@
                             u * K : (u + 1) * K, r * LANES : (r + 1) * LANES
                         ].astype(jnp.float32)
 
-            loop(part // WIDE, step, 2)
+            loop(part // WIDE, step, 4)
 
     def inner_stats(layer):
         acc_in[...] = jnp.zeros_like(acc_in)
@@ -155,7 +156,7 @@
             )
             acc_in[...] += dot(block, block, ((1,), (1,)))
 
-        loop(K // 4, step, 2)
+        loop(K // 4, step, 4)
 
     lane = lax.broadcasted_iota(jnp.int32, (K, LANES), 1)
     sub = lax.broadcasted_iota(jnp.int32, (K, LANES), 0)
@@ -186,9 +187,7 @@
         owner = lax.rem(me + offset + 1, n)
         only(owner < owners, lambda: to_owner(owner).start())
 
-    loop(n - 1, send_tile)
-    forward_beside()
-
+    loop(n - 1, send_tile, spread_out)
     def from_owner(owner, target, index):
         return remote(reduced.at[tile_rows(owner)], reduced.at[tile_rows(owner)], asend.at[index], arecv.at[owner], target)
 
@@ -199,7 +198,7 @@
             source = lax.rem(me + n - offset - 1, n)
             remote(reduce_buf.at[source], reduce_buf.at[source], rsend.at[0], rrecv.at[source], source).wait_recv()
 
-        loop(n - 1, arrive)
+        loop(n - 1, arrive, spread_out)
         total = reduce_buf[0]
         for source in range(1, n):
             total = total + reduce_buf[source]
@@ -208,33 +207,16 @@
         def spread(offset):
             from_owner(me, lax.rem(me + offset + 1, n), offset).start()
 
-        loop(n - 1, spread)
+        loop(n - 1, spread, spread_out)
 
     only(me < owners, reduce_own)
-
-    def arrive_beside(offset):
-        slot = offset * 2 + (1 - mine_c)
-        pass_on(slot, beside, 0).wait_recv()
-
-    loop(n // 2, arrive_beside)
-
-    per_block = LANES // 8
-
-    def turn_queries(index):
-        start = pl.multiple_of(index * LANES, LANES)
-        for block in range(query_blocks):
-            values = gathered[block * per_block : (block + 1) * per_block, :, pl.ds(start, LANES)].astype(jnp.float32)
-            for layer in range(layers):
-                turned = values[:, layer * 8 : (layer + 1) * 8, :].reshape(LANES, LANES).T
-                queries[layer, block, pl.ds(start, LANES), :] = turned.astype(jnp.bfloat16)
-
-    loop(FEATURES // LANES, turn_queries)
+    forward_beside()
 
     def arrive_total(offset):
         owner = lax.rem(me + n - offset - 1, n)
         only(owner < owners, lambda: from_owner(owner, owner, 0).wait_recv())
 
-    loop(n - 1, arrive_total)
+    loop(n - 1, arrive_total, spread_out)
 
     states = []
     for layer in range(layers):
@@ -261,6 +243,24 @@
             new = jnp.where(at_column, column * inverse, value - column * scaled)
             states[layer] = jnp.where(at_row, jnp.where(at_column, -inverse, scaled), new)
 
+    def arrive_beside(offset):
+        slot = offset * 2 + (1 - mine_c)
+        pass_on(slot, beside, 0).wait_recv()
+
+    loop(n // 2, arrive_beside)
+
+    per_block = LANES // 8
+
+    def turn_queries(index):
+        start = pl.multiple_of(index * LANES, LANES)
+        for block in range(query_blocks):
+            values = gathered[block * per_block : (block + 1) * per_block, :, pl.ds(start, LANES)].astype(jnp.float32)
+            for layer in range(layers):
+                turned = values[:, layer * 8 : (layer + 1) * 8, :].reshape(LANES, LANES).T
+                queries[layer, block, pl.ds(start, LANES), :] = turned.astype(jnp.bfloat16)
+
+    loop(FEATURES // LANES, turn_queries, 4)
+
     scores[...] = jnp.zeros_like(scores)
     for layer in range(layers):
         inverse = -states[layer]
@@ -279,7 +279,7 @@
                 for u in range(4):
                     right[pl.ds((index * 4 + u) * PITCH, K), :] = result[:, u * LANES : (u + 1) * LANES]
 
-            loop(K // 4, apply_right, 4)
+            loop(K // 4, apply_right, 8)
 
             def apply_left(index):
                 value = jnp.concatenate(
@@ -291,7 +291,7 @@
                 for u in range(4):
                     both[pl.ds(index * 4 + u, K, stride=PITCH), :] = result[:, u * LANES : (u + 1) * LANES]
 
-            loop(K // 4, apply_left, 4)
+            loop(K // 4, apply_left, 8)
 
             def score(index, layer=layer, block=block):
                 start = pl.multiple_of(index * 1024, 1024)
@@ -312,13 +312,13 @@
         target = lax.rem(me + offset + 1, n)
         remote(power_buf.at[me], power_buf.at[me], psend.at[offset], precv.at[me], target).start()
 
-    loop(n - 1, send_power)
+    loop(n - 1, send_power, spread_out)
 
     def arrive_power(offset):
         source = lax.rem(me + n - offset - 1, n)
         remote(power_buf.at[source], power_buf.at[source], psend.at[0], precv.at[source], source).wait_recv()
 
-    loop(n - 1, arrive_power)
+    loop(n - 1, arrive_power, spread_out)
     power = power_buf[0]
     for source in range(1, n):
         power = power + power_buf[source]
@@ -330,23 +330,23 @@
     def sent_queries(index):
         pass_on(me, beside, index).wait_send()
 
-    loop(n - 1, sent_queries)
+    loop(n - 1, sent_queries, spread_out)
 
     def sent_tile(offset):
         owner = lax.rem(me + offset + 1, n)
         only(owner < owners, lambda: to_owner(owner).wait_send())
 
-    loop(n - 1, sent_tile)
+    loop(n - 1, sent_tile, spread_out)
 
     def sent_total():
-        loop(n - 1, lambda offset: from_owner(me, beside, offset).wait_send())
+        loop(n - 1, lambda offset: from_owner(me, beside, offset).wait_send(), spread_out)
 
     only(me < owners, sent_total)
 
     def sent_power(offset):
         remote(power_buf.at[me], power_buf.at[me], psend.at[offset], precv.at[me], beside).wait_send()
 
-    loop(n - 1, sent_power)
+    loop(n - 1, sent_power, spread_out)
 
 
 def body(train_features, test_features):

time: 57.3 us -> 56.8 us (level)
  Pallas kernels: 55.6 us -> 55 us
    pallas_call x1, Pallas kernels: 55.6 us -> 55 us  [body(): pl.pallas_call(functools.partial(kernel, n, rows * n), out_shape=jax.Shap...]
where the time goes in v3:
time: 56.8 us; the launch traced here: 56.6 us
  Pallas kernels  55 us (97%)
  local copies, waits for them, and re-layouts  1.59 us (3%)
    pallas_call x1, Pallas kernels, body(): pl.pallas_call(functools.partial(kernel, n, rows * n), out_shape=jax.Shap...  55 us
    unnamed x1, local copies, waits for them, and re-layouts  1.59 us

profile of v3, /device:TPU:0, one launch (start us, length us, event | category | flops | bytes accessed | tf_op | source)
XLA Modules:
  0.0 56.6 jit_solution(988152001428751917)
XLA Ops:
  0.0 55.0 %shard_map.28 = bf16[640,128]{1,0:T(8,128)(2,1)} custom-call(bf16[2,640,4096]{2,1,0:T(8,128)(2,1)} %train_hbm.1, bf16[2,8,4096]{2,1,0:T(8,128)(2,1)} %test_ref.1), custom_call_target="tpu_custom_call" | custom-call | tf_op jit(solution)/shard_map/pallas_call | solution.py:361
  55.0 1.6 %copy.4 = bf16[640,128]{1,0:T(8,128)(2,1)} copy(bf16[640,128]{1,0:T(8,128)(2,1)} %shard_map.28) | data formatting | bytes 327680
